TPU v7x, 256 devices: a whole 4x4x8 slice. The times are simulated.
256 devices in a mesh: seq: 32 (over y, x, core), head: 8 (over z).
Axes of the slice: x: 4, y: 4, z: 8, core: 2. Of those that a mesh axis runs over, the one named last changes fastest.
Arguments:
- queries: bfloat16 [16384, 4096], P('seq', 'head'), may hold values from -6 to 6
- keys: bfloat16 [16384, 4096], P('seq', 'head'), may hold values from -6 to 6
- values: bfloat16 [16384, 4096], P('seq', 'head'), may hold values from -48 to 48
- gate_logits: bfloat16 [16384, 4096], P('seq', 'head'), may hold values from -8 to 8
- out_weight: bfloat16 [4096, 6144], P('head'), may hold values from -0.125 to 0.125
Outputs:
- layer_out: bfloat16 [16384, 6144], P('seq', 'head')
All inputs are finite; a program needn't handle non-finite values.
Results may differ from a plain program's by a relative error of at most 0.02.
Values may be sent and summed in bfloat16 or wider, within the bound.
A program may use at most 64 MiB of HBM per device.

v0:
```python
import jax
import jax.numpy as jnp
from jax import lax
from jax.sharding import PartitionSpec as P

HEADS = 32
HEAD_DIM = 128


def activate(raw_input):
    return jax.nn.silu(raw_input.astype(jnp.float32)).astype(jnp.bfloat16)


def body(queries, keys, values, gate_logits, out_weight):
    tokens_here = queries.shape[0]
    feature_count = queries.shape[1]
    heads_here = feature_count // HEAD_DIM
    block_rows = min(512, tokens_here)
    block_count = tokens_here // block_rows
    shape_blocks = (block_count, block_rows, heads_here, HEAD_DIM)
    active_q = activate(queries).reshape(shape_blocks)
    active_k = activate(keys).reshape(shape_blocks)
    active_v = activate(values).reshape(shape_blocks)
    block_states = jnp.einsum(
        "nshd,nshe->nhde", active_k, active_v, preferred_element_type=jnp.float32
    )
    span_total = jnp.sum(block_states, axis=0)
    earlier_local = jnp.cumsum(block_states, axis=0) - block_states
    my_index = lax.axis_index("seq")
    shards = lax.all_gather(
        span_total[None].astype(jnp.bfloat16), "seq", axis=0, tiled=True
    ).astype(jnp.float32)
    positions = jnp.arange(shards.shape[0], dtype=jnp.int32)
    weights = (positions < my_index).astype(jnp.float32)
    prefix = jnp.zeros_like(span_total) + jnp.sum(shards * weights[:, None, None, None], axis=0)
    before = (prefix[None] + earlier_local).astype(jnp.bfloat16)
    causal_mask = jnp.tril(jnp.ones((block_rows, block_rows), jnp.float32))
    scores = jnp.einsum("nthd,nshd->nhts", active_q, active_k, preferred_element_type=jnp.float32)
    scores = (scores * causal_mask).astype(jnp.bfloat16)
    within_block = jnp.einsum(
        "nhts,nshd->nthd", scores, active_v, preferred_element_type=jnp.float32
    )
    from_state = jnp.einsum("nthd,nhde->nthe", active_q, before, preferred_element_type=jnp.float32)
    attended = (within_block + from_state).reshape(tokens_here, feature_count)
    square_sums = lax.psum(jnp.sum(attended * attended, axis=-1), "head")
    scaling = lax.rsqrt(square_sums / (HEADS * HEAD_DIM) + 1e-06)
    gate = jax.nn.sigmoid(gate_logits.astype(jnp.float32))
    normed = (attended * scaling[:, None] * gate).astype(jnp.bfloat16)
    reduced = lax.psum_scatter(
        lax.dot_general(
            out_weight, normed, (((0,), (1,)), ((), ())), preferred_element_type=jnp.float32
        ).astype(jnp.bfloat16),
        "head",
        scatter_dimension=0,
        tiled=True,
    ).astype(jnp.float32)
    return reduced.T.astype(jnp.bfloat16)


def solution(mesh):
    return jax.shard_map(
        body,
        mesh=mesh,
        in_specs=(
            P("seq", "head"),
            P("seq", "head"),
            P("seq", "head"),
            P("seq", "head"),
            P("head", None),
        ),
        out_specs=P("seq", "head"),
        check_vma=False,
    )
```

profile of v0, /device:TPU:1, one launch (start us, length us, event | category | flops | bytes accessed | tf_op | source)
XLA Modules:
  0.0 175.6 jit_solution(14256090123754117991)
XLA Ops:
  6.5 0.0 copy-start
  6.5 0.0 copy-start.1
  6.5 0.0 all-gather.3.cloned.1.call-start
  6.5 1.4 fusion.14
  8.0 0.2 copy.19
  8.2 2.2 %fusion.33 = (bf16[4,128,128]{2,1,0:T(8,128)(2,1)}, f32[4,128,128]{2,1,0:T(8,128)S(1)}) fusion(bf16[512,4,128]{0,2,1:T(8,128)(2,1)S(1)} %bitcast.47, bf16[512,512]{1,0:T(8,128)(2,1)} %param.7), kind=kOutput, calls=%fused_computation.47 | convolution fusion | flops 68747264 | bytes 1441792 | tf_op jit(solution)/shard_map/nshd,nshe->nhde/dot_general | solution.py:24
  10.4 0.0 all-gather.3.cloned.1.call-update
  10.4 0.0 reduce-scatter.2.cloned.1.call-start
  10.5 0.1 fusion.16
  10.6 0.0 copy-done
  10.6 0.0 copy-done.1
  10.6 2.4 %fusion.2 = f32[4,128,512]{2,1,0:T(8,128)} fusion(bf16[512,4,128]{0,2,1:T(8,128)(2,1)S(1)} %bitcast.48, f32[512,512]{1,0:T(8,128)S(1)} %fusion.16, bf16[512,512]{1,0:T(8,128)(2,1)S(1)} %copy-done, bf16[512,512]{1,0:T(8,128)(2,1)S(1)} %copy-done.1), kind=kOutput, calls=%fused_computation.5 | convolution fusion | flops 542113792 | bytes 3670016 | tf_op jit(solution)/shard_map/nhts,nshd->nthd/dot_general | solution.py:40
  13.0 0.0 copy-start.2
  13.0 52.8 %all-gather.3.cloned.1.call-done = bf16[128,128,128]{2,1,0:T(8,128)(2,1)} async-done(((bf16[4,128,128]{2,1,0:T(8,128)(2,1)}), bf16[128,128,128]{2,1,0:T(8,128)(2,1)}) %all-gather.3.cloned.1.call-update) | async-done | bytes 4194320 | tf_op jit(solution)/shard_map/all_gather | solution.py:30
  65.9 3.2 %fusion = f32[4,128,128]{2,1,0:T(8,128)S(1)} fusion(bf16[32,4,128,128]{3,2,1,0:T(8,128)(2,1)} %bitcast.45, f32[32]{0:T(128)S(1)} %compare_convert_fusion), kind=kLoop, calls=%fused_computation.2 | loop fusion | flops 6225920 | bytes 4456576 | tf_op jit(solution)/shard_map/reduce_sum | solution.py:35
  69.1 1.8 %fusion.15 = (f32[512]{0:T(512)S(1)}, f32[4,128,512]{2,1,0:T(8,128)S(1)}) fusion(f32[4,128,512]{2,1,0:T(8,128)} %fusion.2, f32[4,128,128]{2,1,0:T(8,128)S(1)} %fusion, f32[4,128,128]{2,1,0:T(8,128)S(1)} %get-tuple-element.6, bf16[512,512]{1,0:T(8,128)(2,1)S(1)} %copy-done.1), kind=kOutput, calls=%fused_computation.26 | convolution fusion | flops 69664256 | bytes 3147776 | tf_op jit(solution)/shard_map/nthd,nhde->nthe/dot_general | solution.py:43
  70.9 13.9 %psum.7 = f32[512]{0:T(512)S(1)} all-reduce(f32[512]{0:T(512)S(1)} %get-tuple-element.7), channel_id=1, replica_groups=mesh['seq'=32,'head'=8] {'head'}, use_global_device_ids=true, to_apply=%region_2.3 | all-reduce | flops 512 | bytes 4096 | tf_op jit(solution)/shard_map/psum | solution.py:45
  84.7 0.3 copy.17
  85.1 0.0 copy-done.2
  85.1 8.4 %fusion.1 = bf16[6144,512]{0,1:T(8,128)(2,1)} fusion(bf16[512,6144]{1,0:T(8,128)(2,1)} %param.9, bf16[512,512]{1,0:T(8,128)(2,1)S(1)} %copy-done.2, f32[512,512]{1,0:T(8,128)S(1)} %copy.17, f32[512]{0:T(512)S(1)} %add_rsqrt_fusion), kind=kOutput, calls=%fused_computation.3 | convolution fusion | flops 3226206208 | bytes 14157824 | tf_op jit(solution)/shard_map/dot_general | solution.py:50
  93.5 0.0 reduce-scatter.2.cloned.1.call-update
  93.5 75.2 %reduce-scatter.2.cloned.1.call-done = bf16[768,512]{0,1:T(8,128)(2,1)} async-done(((bf16[6144,512]{0,1:T(8,128)(2,1)}), bf16[768,512]{0,1:T(8,128)(2,1)}) %reduce-scatter.2.cloned.1.call-update) | async-done | bytes 786448 | tf_op jit(solution)/shard_map/reduce_scatter | solution.py:49
  (2 shorter events, 0.0 us)
Async XLA Ops:
  6.5 4.1 %copy-start = (bf16[512,512]{1,0:T(8,128)(2,1)S(1)}, bf16[512,512]{1,0:T(8,128)(2,1)}, u32[]{:S(2)}) copy-start(bf16[512,512]{1,0:T(8,128)(2,1)} %param.7) | copy-start | bytes 1572868
  6.5 4.1 %copy-start.1 = (bf16[512,512]{1,0:T(8,128)(2,1)S(1)}, bf16[512,512]{1,0:T(8,128)(2,1)}, u32[]{:S(2)}) copy-start(bf16[512,512]{1,0:T(8,128)(2,1)} %param.5) | copy-start | bytes 1572868
  6.5 59.3 %all-gather.3.cloned.1.call-start = ((), (), s32[]{:S(2)}) async-start(), calls=%async_computation.2 | async-start | bytes 4325376 | tf_op jit(solution)/shard_map/all_gather | solution.py:30
  10.4 158.4 %reduce-scatter.2.cloned.1.call-start = ((), (), s32[]{:S(2)}) async-start(), calls=%async_computation.1 | async-start | bytes 7077888 | tf_op jit(solution)/shard_map/reduce_scatter | solution.py:49
  13.0 72.0 %copy-start.2 = (bf16[512,512]{1,0:T(8,128)(2,1)S(1)}, bf16[512,512]{1,0:T(8,128)(2,1)}, u32[]{:S(2)}) copy-start(bf16[512,512]{1,0:T(8,128)(2,1)} %param.8) | copy-start | bytes 1572868
Sparse Core Ops, SparseCore 0:
  10.5 55.2 all-gather.2
  93.7 75.0 reduce-scatter.1
where the time goes:
time: 176 us
  waiting for transfers between devices  128 us (73%)
  matrix products  14.8 us (8%)
  blocking collectives  13.9 us (8%)
  between operations  13.5 us (8%)
  other arithmetic  4.77 us (3%)
    reduce_scatter x1, waiting for transfers between devices, body(): lax.psum_scatter(lax.dot_general(out_weight, normed, (((0,), (1,)), ((),...  75.2 us
    all_gather x1, waiting for transfers between devices, body(): lax.all_gather(span_total[None].astype(jnp.bfloat16), 'seq', axis=0, tile...  52.8 us
    psum x1, blocking collectives, body(): square_sums = lax.psum(jnp.sum(attended * attended, axis=-1), 'head')  13.9 us
    dot_general x1, matrix products, body(): lax.dot_general(out_weight, normed, (((0,), (1,)), ((), ())), preferred_e...  8.42 us
  transfers between devices with their start and end apart: 2, of which 2 were waited for; matrix products, arithmetic and copies ran while one was open for 1% of the time, Pallas kernels for 0%

commit v1 on v0

v1 whole, which is shorter than its diff:
```python
import functools

import jax
import jax.numpy as jnp
from jax import lax
from jax.experimental import pallas as pl
from jax.experimental.pallas import tpu as pltpu
from jax.sharding import PartitionSpec as P

HEADS = 32
HEAD_DIM = 128
F32 = jnp.float32
BF16 = jnp.bfloat16
MESH = pl.DeviceIdType.MESH

NX = 4
NZ = 8
ROWS = 512
FEAT = 512
OUT = 768
CHUNK = 128
NCHUNK = ROWS // CHUNK
HALF = OUT // 2


def sigmoid(value):
    return 0.5 + 0.5 * jnp.tanh(0.5 * value)


def silu(raw):
    value = raw.astype(F32)
    return (value * sigmoid(value)).astype(BF16)


def contract(lhs, rhs, lhs_dim, rhs_dim):
    return lax.dot_general(
        lhs, rhs, (((lhs_dim,), (rhs_dim,)), ((), ())), preferred_element_type=F32
    )


def kernel(
    q_hbm, k_hbm, v_hbm, g_hbm, w_hbm, out_ref,
    q_in, k_in, v_in, g_in, aq, ak, av, within, gate,
    s_full, s_bf, sib, tot_bf, arr_a, pay, arr_b, back, state,
    gathered, weight, acc, ss_own, ss_all,
    load_sem, z_send, z_recv, p_send, p_recv, a_send, a_recv, b_send, b_recv,
    ss_send, ss_recv, r_send, r_recv, l_send, l_recv,
    wa_send, wa_recv, wb_send, wb_recv, ws_send, ws_recv,
):
    seq = lax.axis_index("seq")
    z = lax.axis_index("head")
    c = lax.rem(seq, 2)
    x = lax.rem(lax.div(seq, 2), NX)
    y = lax.div(seq, 2 * NX)
    a = x * (1 - c) + y * c
    b = y * (1 - c) + x * c

    def on_plane(a2, b2):
        x2 = a2 * (1 - c) + b2 * c
        y2 = b2 * (1 - c) + a2 * c
        return ((y2 * NX + x2) * 2 + c, z)

    def a_peer(step):
        return on_plane(lax.rem(a + step, NX), b)

    def b_peer(step):
        return on_plane(a, lax.rem(b + step, NX))

    def z_peer(step):
        return (seq, lax.rem(z + step, NZ))

    sibling = (seq + 1 - 2 * c, z)

    def remote(src, dst, send_sem, recv_sem, device):
        return pltpu.make_async_remote_copy(
            src_ref=src, dst_ref=dst, send_sem=send_sem, recv_sem=recv_sem,
            device_id=device, device_id_type=MESH,
        )

    barrier = pltpu.get_barrier_semaphore()
    partners = (
        [sibling]
        + [a_peer(step) for step in range(1, NX)]
        + [b_peer(step) for step in range(1, NX)]
        + [z_peer(step) for step in range(1, NZ)]
    )
    for partner in partners:
        pl.semaphore_signal(barrier, inc=1, device_id=partner, device_id_type=MESH)

    def load(src, dst, index):
        copy = pltpu.make_async_copy(src, dst, load_sem.at[index])
        copy.start()
        return copy

    load_k = load(k_hbm, k_in, 0)
    load_v = load(v_hbm, v_in, 1)
    load_q = load(q_hbm, q_in, 2)
    load_g = load(g_hbm, g_in, 3)
    own_columns = pl.ds(pl.multiple_of(z * OUT, 128), OUT)
    load_w = load(w_hbm.at[:, own_columns], weight.at[0], 4)

    def head(h):
        return slice(h * HEAD_DIM, (h + 1) * HEAD_DIM)

    load_k.wait()
    load_v.wait()
    for h in range(4):
        ak[:, head(h)] = silu(k_in[:, head(h)])
        av[:, head(h)] = silu(v_in[:, head(h)])
        outer = contract(ak[:, head(h)], av[:, head(h)], 0, 0)
        s_full[h] = outer
        s_bf[h] = outer.astype(BF16)

    pl.semaphore_wait(barrier, len(partners))

    mine = pl.ds(c * 2, 2)
    first = remote(
        s_bf.at[pl.ds((1 - c) * 2, 2)], sib, p_send.at[0], p_recv.at[0], sibling
    )
    first.start()

    share = pl.multiple_of(c * 256 + b * 64 + a * 16, 16)
    weight_z = []
    for step in range(1, NZ):
        columns = pl.ds(pl.multiple_of(lax.rem(z + step, NZ) * OUT, 128), OUT)
        copy = remote(
            w_hbm.at[pl.ds(share, 16), columns],
            weight.at[NZ - step, pl.ds(share, 16)],
            z_send.at[step - 1], z_recv.at[step - 1], z_peer(step),
        )
        copy.start()
        weight_z.append(copy)

    load_q.wait()
    for h in range(4):
        aq[:, head(h)] = silu(q_in[:, head(h)])

    first.wait_recv()
    total = s_full[mine] + sib[...].astype(F32)
    tot_bf[...] = total.astype(BF16)

    phase_a = []
    for step in range(1, NX):
        copy = remote(
            tot_bf, arr_a.at[step - 1], a_send.at[step - 1], a_recv.at[step - 1], a_peer(step)
        )
        copy.start()
        phase_a.append(copy)

    half = ROWS // 2
    row_id = lax.broadcasted_iota(jnp.int32, (half, half), 0)
    col_id = lax.broadcasted_iota(jnp.int32, (half, half), 1)
    causal = row_id >= col_id

    def attend_block(h):
        for part in range(2):
            rows = slice(part * half, (part + 1) * half)
            qh = aq[rows, head(h)]
            diag = contract(qh, ak[rows, head(h)], 1, 1)
            diag = jnp.where(causal, diag, 0.0).astype(BF16)
            result = contract(diag, av[rows, head(h)], 1, 0)
            if part == 1:
                low = contract(qh, ak[0:half, head(h)], 1, 1).astype(BF16)
                result = result + contract(low, av[0:half, head(h)], 1, 0)
            within[rows, head(h)] = result

    attend_block(0)
    attend_block(1)

    for copy in phase_a:
        copy.wait_recv()
    total = s_full[mine] + sib[...].astype(F32)
    low_sum = jnp.zeros((2, HEAD_DIM, HEAD_DIM), F32)
    all_sum = total
    for step in range(1, NX):
        term = arr_a[step - 1].astype(F32)
        low_sum = low_sum + term * jnp.where(a >= step, 1.0, 0.0).astype(F32)
        all_sum = all_sum + term
    core0 = jnp.where(c == 0, 1.0, 0.0).astype(F32)
    core1 = 1.0 - core0
    pay[0] = (core0 * all_sum + core1 * (low_sum + total)).astype(BF16)
    pay[1] = (core1 * low_sum).astype(BF16)

    phase_b = []
    for step in range(1, NX):
        copy = remote(
            pay.at[lax.div(b + step, NX)], arr_b.at[step - 1],
            b_send.at[step - 1], b_recv.at[step - 1], b_peer(step),
        )
        copy.start()
        phase_b.append(copy)

    attend_block(2)
    attend_block(3)
    load_g.wait()
    for h in range(4):
        gate[:, head(h)] = sigmoid(g_in[:, head(h)].astype(F32))

    low_sum = jnp.zeros((2, HEAD_DIM, HEAD_DIM), F32)
    for step in range(1, NX):
        low_sum = low_sum + arr_a[step - 1].astype(F32) * jnp.where(a >= step, 1.0, 0.0).astype(F32)
    for copy in phase_b:
        copy.wait_recv()
    for step in range(1, NX):
        low_sum = low_sum + arr_b[step - 1].astype(F32)
    back[...] = (low_sum + core0 * s_full[mine]).astype(BF16)
    last = remote(back, state.at[mine], p_send.at[1], p_recv.at[1], sibling)
    last.start()
    state[mine] = (low_sum + core1 * sib[...].astype(F32)).astype(BF16)

    others = pl.ds(1, NZ - 1)
    for copy in weight_z:
        copy.wait_recv()

    def share_rows(step):
        return pl.ds(pl.multiple_of(c * 256 + b * 64 + lax.rem(a + step, NX) * 16, 16), 16)

    def group_rows(step):
        return pl.ds(pl.multiple_of(c * 256 + lax.rem(b + step, NX) * 64, 64), 64)

    def ring_starts(rows, peer, send_sem, recv_sem):
        piece = weight.at[others, rows(0)]
        up = remote(piece, piece, send_sem.at[0], recv_sem.at[0], peer(1))
        down = remote(piece, piece, send_sem.at[1], recv_sem.at[1], peer(NX - 1))
        up.start()
        down.start()
        return [up, down]

    def ring_forwards(rows, peer, send_sem, recv_sem, copies):
        copies[0].wait_recv()
        from_below = weight.at[others, rows(NX - 1), pl.ds(0, HALF)]
        up = remote(from_below, from_below, send_sem.at[2], recv_sem.at[2], peer(1))
        up.start()
        copies[1].wait_recv()
        from_above = weight.at[others, rows(1), pl.ds(HALF, HALF)]
        down = remote(from_above, from_above, send_sem.at[3], recv_sem.at[3], peer(NX - 1))
        down.start()
        return [up, down]

    ring_a = ring_starts(share_rows, a_peer, wa_send, wa_recv)

    last.wait_recv()

    def slot_send(index, hop, chunk, up):
        rows = pl.ds(pl.multiple_of(chunk * CHUNK, CHUNK), CHUNK)
        if up:
            src, dst = lax.rem(NZ + 1 - hop, NZ), NZ - hop
            return remote(
                gathered.at[src, rows], gathered.at[dst, rows],
                r_send.at[index], r_recv.at[index], z_peer(1),
            )
        return remote(
            gathered.at[hop - 1, rows], gathered.at[hop, rows],
            l_send.at[index], l_recv.at[index], z_peer(NZ - 1),
        )

    ss_own[...] = jnp.zeros_like(ss_own)
    for chunk in range(NCHUNK):
        rows = slice(chunk * CHUNK, (chunk + 1) * CHUNK)
        squares = jnp.zeros((CHUNK, HEAD_DIM), F32)
        for h in range(4):
            att = within[rows, head(h)] + contract(aq[rows, head(h)], state[h], 1, 0)
            squares = squares + att * att
            gathered[0, rows, head(h)] = (att * gate[rows, head(h)]).astype(BF16)
        slot_send(chunk, 1, chunk, True).start()
        slot_send(chunk, 1, chunk, False).start()
        ss_own[chunk : chunk + 1, :] = jnp.sum(squares.T, axis=0, keepdims=True)

    square_sends = []
    for step in range(1, NZ):
        copy = remote(
            ss_own, ss_all.at[step - 1], ss_send.at[step - 1], ss_recv.at[step - 1], z_peer(step)
        )
        copy.start()
        square_sends.append(copy)

    def project(slot, row, count, fresh=False):
        rows = pl.ds(pl.multiple_of(row, CHUNK), count)
        for n in range(OUT // 256):
            cols = slice(n * 256, (n + 1) * 256)
            term = jnp.dot(
                gathered[slot, rows, :], weight[slot, :, cols], preferred_element_type=F32
            )
            if fresh:
                acc[rows, cols] = term
            else:
                acc[rows, cols] += term

    load_w.wait()
    for part in range(2):
        project(0, part * 256, 256, fresh=True)

    def pass_on(index, _):
        hop = lax.div(index, NCHUNK) + 1
        chunk = lax.rem(index, NCHUNK)
        slot_send(index, hop, chunk, True).wait_recv()
        slot_send(index + NCHUNK, hop + 1, chunk, True).start()
        slot_send(index, hop, chunk, False).wait_recv()
        slot_send(index + NCHUNK, hop + 1, chunk, False).start()
        return 0

    def pass_range(start, stop):
        lax.fori_loop(start, stop, pass_on, 0)

    pass_range(0, 1)
    ring_a2 = ring_forwards(share_rows, a_peer, wa_send, wa_recv, ring_a)
    pass_range(1, 2)
    for copy in ring_a2:
        copy.wait_recv()
    ring_b = ring_starts(group_rows, b_peer, wb_send, wb_recv)

    def to_sibling(step):
        piece = weight.at[others, group_rows(step)]
        copy = remote(piece, piece, ws_send.at[step], ws_recv.at[step], sibling)
        copy.start()
        return copy

    sibling_sends = [to_sibling(0)]
    pass_range(2, 5)
    ring_b2 = ring_forwards(group_rows, b_peer, wb_send, wb_recv, ring_b)
    sibling_sends.append(to_sibling(1))
    sibling_sends.append(to_sibling(3))
    pass_range(5, 7)
    for copy in ring_b2:
        copy.wait_recv()
    sibling_sends.append(to_sibling(2))
    pass_range(7, 8)
    for copy in sibling_sends:
        copy.wait_recv()

    def hop_three(chunk):
        index = 2 * NCHUNK + chunk
        slot_send(index, 3, chunk, True).wait_recv()
        if chunk < NCHUNK // 2:
            slot_send(index + NCHUNK, 4, chunk, True).start()
        slot_send(index, 3, chunk, False).wait_recv()
        if chunk >= NCHUNK // 2:
            slot_send(index + NCHUNK, 4, chunk, False).start()

    def project_whole(slot):
        def body(part, _):
            project(slot, part * 256, 256)
            return 0
        lax.fori_loop(0, 2, body, 0)

    hop_three(0)
    project_whole(7)
    hop_three(1)
    project_whole(1)
    hop_three(2)
    project_whole(6)
    hop_three(3)
    project_whole(2)
    project_whole(5)
    project_whole(3)

    for step in range(NZ - 1):
        square_sends[step].wait_recv()
    sums = ss_own[...]
    for step in range(NZ - 1):
        sums = sums + ss_all[step]
    factor = lax.rsqrt(sums / (HEADS * HEAD_DIM) + 1e-06)

    for pair in range(NCHUNK // 2):
        for chunk, up in ((pair, True), (pair + NCHUNK // 2, False)):
            slot_send(3 * NCHUNK + chunk, 4, chunk, up).wait_recv()
            project(4, chunk * CHUNK, CHUNK)
            rows = slice(chunk * CHUNK, (chunk + 1) * CHUNK)
            column = jnp.broadcast_to(factor[chunk : chunk + 1, :], (CHUNK, CHUNK)).T
            for n in range(OUT // 128):
                cols = slice(n * 128, (n + 1) * 128)
                out_ref[rows, cols] = (acc[rows, cols] * column).astype(BF16)

    first.wait_send()
    last.wait_send()
    for copy in (
        weight_z + phase_a + phase_b + square_sends
        + ring_a + ring_a2 + ring_b + ring_b2 + sibling_sends
    ):
        copy.wait_send()

    def drain(index, _):
        hop = lax.div(index, NCHUNK) + 1
        chunk = lax.rem(index, NCHUNK)
        slot_send(index, hop, chunk, True).wait_send()
        slot_send(index, hop, chunk, False).wait_send()
        return 0

    lax.fori_loop(0, 3 * NCHUNK, drain, 0)
    for chunk in range(NCHUNK):
        slot_send(3 * NCHUNK + chunk, 4, chunk, chunk < NCHUNK // 2).wait_send()


def body(queries, keys, values, gate_logits, out_weight):
    dma = pltpu.SemaphoreType.DMA
    pair = (2, HEAD_DIM, HEAD_DIM)
    vmem = pltpu.VMEM
    return pl.pallas_call(
        kernel,
        out_shape=jax.ShapeDtypeStruct((ROWS, OUT), BF16),
        in_specs=[pl.BlockSpec(memory_space=pl.ANY)] * 5,
        out_specs=pl.BlockSpec(memory_space=pltpu.VMEM),
        scratch_shapes=[
            vmem((ROWS, FEAT), BF16), vmem((ROWS, FEAT), BF16),
            vmem((ROWS, FEAT), BF16), vmem((ROWS, FEAT), BF16),
            vmem((ROWS, FEAT), BF16), vmem((ROWS, FEAT), BF16), vmem((ROWS, FEAT), BF16),
            vmem((ROWS, FEAT), F32), vmem((ROWS, FEAT), F32),
            vmem((4, HEAD_DIM, HEAD_DIM), F32), vmem((4, HEAD_DIM, HEAD_DIM), BF16),
            vmem(pair, BF16), vmem(pair, BF16), vmem((NX - 1,) + pair, BF16),
            vmem((2,) + pair, BF16), vmem((NX - 1,) + pair, BF16),
            vmem(pair, BF16), vmem((4, HEAD_DIM, HEAD_DIM), BF16),
            vmem((NZ, ROWS, FEAT), BF16), vmem((NZ, ROWS, OUT), BF16),
            vmem((ROWS, OUT), F32), vmem((8, 128), F32), vmem((NZ - 1, 8, 128), F32),
            dma((5,)), dma((NZ - 1,)), dma((NZ - 1,)), dma((2,)), dma((2,)),
            dma((NX - 1,)), dma((NX - 1,)), dma((NX - 1,)), dma((NX - 1,)),
            dma((NZ - 1,)), dma((NZ - 1,)),
            dma((4 * NCHUNK,)), dma((4 * NCHUNK,)), dma((4 * NCHUNK,)), dma((4 * NCHUNK,)),
            dma((4,)), dma((4,)), dma((4,)), dma((4,)), dma((4,)), dma((4,)),
        ],
        compiler_params=pltpu.CompilerParams(
            collective_id=0, has_side_effects=True, vmem_limit_bytes=48 * 1024 * 1024
        ),
        cost_estimate=pl.CostEstimate(
            flops=3_900_000_000, bytes_accessed=9_000_000, transcendentals=1_000_000
        ),
    )(queries, keys, values, gate_logits, out_weight)


def solution(mesh):
    return jax.shard_map(
        body,
        mesh=mesh,
        in_specs=(
            P("seq", "head"),
            P("seq", "head"),
            P("seq", "head"),
            P("seq", "head"),
            P("head", None),
        ),
        out_specs=P("seq", "head"),
        check_vma=False,
    )
```

time: 176 us -> 71.2 us (0.40)
  waiting for transfers between devices: 128 us -> 0 us
  Pallas kernels: 0 us -> 65.8 us
  matrix products: 14.8 us -> 0 us
  blocking collectives: 13.9 us -> 0 us
  between operations: 13.5 us -> 0.01 us
  other arithmetic: 4.77 us -> 0 us
  local copies, waits for them, and re-layouts: 0.56 us -> 5.05 us
    reduce_scatter x1 -> x0, waiting for transfers between devices: 75.2 us -> none  [body(): lax.psum_scatter(lax.dot_general(out_weight, normed, (((0,), (1,)), ((),...]
    pallas_call x0 -> x1, Pallas kernels: none -> 65.8 us  [body(): pl.pallas_call(kernel, out_shape=jax.ShapeDtypeStruct((ROWS, OUT), BF16),...]
    all_gather x1 -> x0, waiting for transfers between devices: 52.8 us -> none  [body(): lax.all_gather(span_total[None].astype(jnp.bfloat16), 'seq', axis=0, tile...]
    dot_general x4 -> x0, matrix products: 14.8 us -> none  [the longest x1 8.42 us: body(): lax.dot_general(out_weight, normed, (((0,), (1,)), ((), ())), preferred_e...]
    psum x1 -> x0, blocking collectives: 13.9 us -> none  [body(): square_sums = lax.psum(jnp.sum(attended * attended, axis=-1), 'head')]
    unnamed x6 -> x9, local copies, waits for them, and re-layouts: 0.01 us -> 5.05 us
    reduce_sum x1 -> x0, other arithmetic: 3.21 us -> none  [body(): jnp.sum(shards * weights[:, None, None, None], axis=0)]
  transfers between devices with their start and end apart: 2 -> 0, of which waited for: 2 -> 0; matrix products, arithmetic and copies ran while one was open for 1% -> 0% of each run, Pallas kernels for 0% -> 0%
where the time goes in v1:
time: 71.2 us; the launch traced here: 70.9 us
  Pallas kernels  65.8 us (92%)
  local copies, waits for them, and re-layouts  5.05 us (7%)
    pallas_call x1, Pallas kernels, body(): pl.pallas_call(kernel, out_shape=jax.ShapeDtypeStruct((ROWS, OUT), BF16),...  65.8 us
    unnamed x9, local copies, waits for them, and re-layouts  5.05 us

profile of v1, /device:TPU:1, one launch (start us, length us, event | category | flops | bytes accessed | tf_op | source)
XLA Modules:
  0.0 70.9 jit_solution(10023246086684571487)
XLA Ops:
  0.0 0.0 copy-start
  0.0 1.0 %copy-done = bf16[512,512]{1,0:T(8,128)(2,1)S(1)} copy-done((bf16[512,512]{1,0:T(8,128)(2,1)S(1)}, bf16[512,512]{1,0:T(8,128)(2,1)}, u32[]{:S(2)}) %copy-start) | copy-done | bytes 524312
  1.0 0.0 copy-start.1
  1.0 1.0 %copy-done.1 = bf16[512,512]{1,0:T(8,128)(2,1)S(1)} copy-done((bf16[512,512]{1,0:T(8,128)(2,1)S(1)}, bf16[512,512]{1,0:T(8,128)(2,1)}, u32[]{:S(2)}) %copy-start.1) | copy-done | bytes 524312
  2.1 0.0 copy-start.2
  2.1 1.0 %copy-done.2 = bf16[512,512]{1,0:T(8,128)(2,1)S(1)} copy-done((bf16[512,512]{1,0:T(8,128)(2,1)S(1)}, bf16[512,512]{1,0:T(8,128)(2,1)}, u32[]{:S(2)}) %copy-start.2) | copy-done | bytes 524312
  3.1 0.0 copy-start.3
  3.1 1.0 %copy-done.3 = bf16[512,512]{1,0:T(8,128)(2,1)S(1)} copy-done((bf16[512,512]{1,0:T(8,128)(2,1)S(1)}, bf16[512,512]{1,0:T(8,128)(2,1)}, u32[]{:S(2)}) %copy-start.3) | copy-done | bytes 524312
  4.2 65.8 %shard_map.55 = bf16[512,768]{1,0:T(8,128)(2,1)S(1)} custom-call(bf16[512,512]{1,0:T(8,128)(2,1)S(1)} %copy-done, bf16[512,512]{1,0:T(8,128)(2,1)S(1)} %copy-done.1, bf16[512,512]{1,0:T(8,128)(2,1)S(1)} %copy-done.2, bf16[512,512]{1,0:T(8,128)(2,1)S(1)} %copy-done.3, bf16[512,6144]{1,0:T(8,128)(2,1)} %w_hbm.1), custom_call_target="tpu_custom_call" | custom-call | flops 3900000000 | bytes 9000000 | tf_op jit(solution)/shard_map/pallas_call | solution.py:398
  70.0 0.9 %copy.7 = bf16[512,768]{1,0:T(8,128)(2,1)} copy(bf16[512,768]{1,0:T(8,128)(2,1)S(1)} %shard_map.55) | data formatting | bytes 1572864
Async XLA Ops:
  0.0 1.0 %copy-start = (bf16[512,512]{1,0:T(8,128)(2,1)S(1)}, bf16[512,512]{1,0:T(8,128)(2,1)}, u32[]{:S(2)}) copy-start(bf16[512,512]{1,0:T(8,128)(2,1)} %q_hbm.1) | copy-start | bytes 1572868
  1.0 1.0 %copy-start.1 = (bf16[512,512]{1,0:T(8,128)(2,1)S(1)}, bf16[512,512]{1,0:T(8,128)(2,1)}, u32[]{:S(2)}) copy-start(bf16[512,512]{1,0:T(8,128)(2,1)} %k_hbm.1) | copy-start | bytes 1572868
  2.1 1.0 %copy-start.2 = (bf16[512,512]{1,0:T(8,128)(2,1)S(1)}, bf16[512,512]{1,0:T(8,128)(2,1)}, u32[]{:S(2)}) copy-start(bf16[512,512]{1,0:T(8,128)(2,1)} %v_hbm.1) | copy-start | bytes 1572868
  3.1 1.0 %copy-start.3 = (bf16[512,512]{1,0:T(8,128)(2,1)S(1)}, bf16[512,512]{1,0:T(8,128)(2,1)}, u32[]{:S(2)}) copy-start(bf16[512,512]{1,0:T(8,128)(2,1)} %g_hbm.1) | copy-start | bytes 1572868

commit v2 on v1

v2 whole, which is shorter than its diff:
```python
import functools

import jax
import jax.numpy as jnp
from jax import lax
from jax.experimental import pallas as pl
from jax.experimental.pallas import tpu as pltpu
from jax.sharding import PartitionSpec as P

HEADS = 32
HEAD_DIM = 128
F32 = jnp.float32
BF16 = jnp.bfloat16
MESH = pl.DeviceIdType.MESH

NX = 4
NZ = 8
ROWS = 512
FEAT = 512
OUT = 768
PAIR = 256
NCHUNK = 4
HALF = OUT // 2


def sigmoid(value):
    return 0.5 + 0.5 * jnp.tanh(0.5 * value)


def silu(raw):
    value = raw.astype(F32)
    return (value * sigmoid(value)).astype(BF16)


def contract(lhs, rhs, lhs_dim, rhs_dim):
    return lax.dot_general(
        lhs, rhs, (((lhs_dim,), (rhs_dim,)), ((), ())), preferred_element_type=F32
    )


def kernel(
    q_hbm, k_hbm, v_hbm, g_hbm, w_hbm, out_ref,
    q_in, k_in, v_in, g_in, aq, ak, av, within, gate, squares,
    s_full, s_bf, sib, tot_bf, low_sum, arr_a, pay, arr_b, back, state,
    gathered, weight, acc, ss_own, ss_all,
    load_sem, z_send, z_recv, p_send, p_recv, a_send, a_recv, b_send, b_recv,
    ss_send, ss_recv, r_send, r_recv, l_send, l_recv,
    wa_send, wa_recv, wb_send, wb_recv, ws_send, ws_recv,
):
    seq = lax.axis_index("seq")
    z = lax.axis_index("head")
    c = lax.rem(seq, 2)
    x = lax.rem(lax.div(seq, 2), NX)
    y = lax.div(seq, 2 * NX)
    a = x * (1 - c) + y * c
    b = y * (1 - c) + x * c

    def chip(x_step, y_step):
        x2 = lax.rem(x + x_step, NX)
        y2 = lax.rem(y + y_step, NX)
        return ((y2 * NX + x2) * 2 + c, z)

    def a_peer(step):
        return chip(step * (1 - c), step * c)

    def b_peer(step):
        return chip(step * c, step * (1 - c))

    def z_peer(step):
        return (seq, lax.rem(z + step, NZ))

    sibling = (seq + 1 - 2 * c, z)

    def remote(src, dst, send_sem, recv_sem, device):
        return pltpu.make_async_remote_copy(
            src_ref=src, dst_ref=dst, send_sem=send_sem, recv_sem=recv_sem,
            device_id=device, device_id_type=MESH,
        )

    barrier = pltpu.get_barrier_semaphore()
    partners = (
        [sibling]
        + [chip(step, 0) for step in range(1, NX)]
        + [chip(0, step) for step in range(1, NX)]
        + [z_peer(step) for step in range(1, NZ)]
    )
    for partner in partners:
        pl.semaphore_signal(barrier, inc=1, device_id=partner, device_id_type=MESH)

    def load(src, dst, index):
        copy = pltpu.make_async_copy(src, dst, load_sem.at[index])
        copy.start()
        return copy

    def head(h):
        return slice(h * HEAD_DIM, (h + 1) * HEAD_DIM)

    loads_kv = []
    for stage in range(2):
        part = pl.ds(stage * PAIR, PAIR)
        loads_kv.append((
            load(k_hbm.at[:, part], k_in.at[:, part], 2 * stage),
            load(v_hbm.at[:, part], v_in.at[:, part], 2 * stage + 1),
        ))
    load_q = load(q_hbm, q_in, 4)
    load_g = load(g_hbm, g_in, 5)
    own_columns = pl.ds(pl.multiple_of(z * OUT, 128), OUT)
    load_w = load(w_hbm.at[:, own_columns], weight.at[0], 6)

    def stage_heads(stage):
        return pl.ds(2 * stage, 2)

    def to_core1(stage):
        return remote(
            s_bf.at[stage_heads(stage)], sib.at[stage_heads(stage)],
            p_send.at[stage], p_recv.at[stage], sibling,
        )

    def to_core0(stage):
        return remote(
            back.at[stage_heads(stage)], state.at[stage_heads(stage)],
            p_send.at[2 + stage], p_recv.at[2 + stage], sibling,
        )

    def first_phase(h, step):
        index = h * (NX - 1) + step - 1
        device = chip(step, 0) if h % 2 == 0 else chip(0, step)
        return remote(
            tot_bf.at[h], arr_a.at[h, step - 1], a_send.at[index], a_recv.at[index], device
        )

    def second_phase(h, step):
        index = h * (NX - 1) + step - 1
        device = chip(0, step) if h % 2 == 0 else chip(step, 0)
        place = y if h % 2 == 0 else x
        return remote(
            pay.at[h, lax.div(place + step, NX)], arr_b.at[h, step - 1],
            b_send.at[index], b_recv.at[index], device,
        )

    def local_states(stage):
        for copy in loads_kv[stage]:
            copy.wait()
        for h in (2 * stage, 2 * stage + 1):
            ak[:, head(h)] = silu(k_in[:, head(h)])
            av[:, head(h)] = silu(v_in[:, head(h)])
            outer = contract(ak[:, head(h)], av[:, head(h)], 0, 0)
            s_full[h] = outer
            s_bf[h] = outer.astype(BF16)

    local_states(0)
    pl.semaphore_wait(barrier, len(partners))
    pl.when(c == 0)(lambda: to_core1(0).start())
    local_states(1)
    pl.when(c == 0)(lambda: to_core1(1).start())

    @pl.when(c == 1)
    def _():
        for stage in range(2):
            to_core1(stage).wait_recv()
            for h in (2 * stage, 2 * stage + 1):
                tot_bf[h] = (s_full[h] + sib[h].astype(F32)).astype(BF16)
                for step in range(1, NX):
                    first_phase(h, step).start()

    share = pl.multiple_of(c * 256 + b * 64 + a * 16, 16)
    weight_z = []
    for step in range(1, NZ):
        columns = pl.ds(pl.multiple_of(lax.rem(z + step, NZ) * OUT, 128), OUT)
        copy = remote(
            w_hbm.at[pl.ds(share, 16), columns],
            weight.at[NZ - step, pl.ds(share, 16)],
            z_send.at[step - 1], z_recv.at[step - 1], z_peer(step),
        )
        copy.start()
        weight_z.append(copy)

    half = ROWS // 2
    row_id = lax.broadcasted_iota(jnp.int32, (half, half), 0)
    col_id = lax.broadcasted_iota(jnp.int32, (half, half), 1)
    causal = row_id >= col_id

    def attend_block(h):
        for part in range(2):
            rows = slice(part * half, (part + 1) * half)
            qh = aq[rows, head(h)]
            diag = contract(qh, ak[rows, head(h)], 1, 1)
            diag = jnp.where(causal, diag, 0.0).astype(BF16)
            result = contract(diag, av[rows, head(h)], 1, 0)
            if part == 1:
                low = contract(qh, ak[0:half, head(h)], 1, 1).astype(BF16)
                result = result + contract(low, av[0:half, head(h)], 1, 0)
            within[rows, head(h)] = result

    load_q.wait()
    for h in range(4):
        aq[:, head(h)] = silu(q_in[:, head(h)])
    attend_block(0)
    attend_block(1)

    def turn(stage):
        for h in (2 * stage, 2 * stage + 1):
            place = x if h % 2 == 0 else y
            total = s_full[h] + sib[h].astype(F32)
            lower = jnp.zeros((HEAD_DIM, HEAD_DIM), F32)
            whole = total
            for step in range(1, NX):
                first_phase(h, step).wait_recv()
                term = arr_a[h, step - 1].astype(F32)
                lower = lower + term * jnp.where(place >= step, 1.0, 0.0).astype(F32)
                whole = whole + term
            low_sum[h] = lower
            if h % 2 == 0:
                pay[h, 0] = whole.astype(BF16)
                pay[h, 1] = jnp.zeros((HEAD_DIM, HEAD_DIM), BF16)
            else:
                pay[h, 0] = (lower + total).astype(BF16)
                pay[h, 1] = lower.astype(BF16)
            for step in range(1, NX):
                second_phase(h, step).start()

    pl.when(c == 1)(lambda: turn(0))
    attend_block(2)
    pl.when(c == 1)(lambda: turn(1))
    attend_block(3)
    load_g.wait()
    for h in range(4):
        gate[:, head(h)] = sigmoid(g_in[:, head(h)].astype(F32))

    def finish_state(stage):
        @pl.when(c == 1)
        def _():
            for h in (2 * stage, 2 * stage + 1):
                before = low_sum[h]
                for step in range(1, NX):
                    second_phase(h, step).wait_recv()
                    before = before + arr_b[h, step - 1].astype(F32)
                back[h] = before.astype(BF16)
                state[h] = (before + sib[h].astype(F32)).astype(BF16)
            to_core0(stage).start()

        @pl.when(c == 0)
        def _():
            to_core0(stage).wait_recv()

    def slot_send(index, hop, chunk, up):
        part = lax.div(chunk, 2)
        rows = pl.ds(pl.multiple_of(lax.rem(chunk, 2) * half, half), half)
        if up:
            src, dst = lax.rem(NZ + 1 - hop, NZ), NZ - hop
            return remote(
                gathered.at[src, part, rows], gathered.at[dst, part, rows],
                r_send.at[index], r_recv.at[index], z_peer(1),
            )
        return remote(
            gathered.at[hop - 1, part, rows], gathered.at[hop, part, rows],
            l_send.at[index], l_recv.at[index], z_peer(NZ - 1),
        )

    def finish_attended(stage):
        for part in range(2):
            rows = slice(part * half, (part + 1) * half)
            total = jnp.zeros((half, HEAD_DIM), F32) if stage == 0 else squares[rows, :]
            for i in range(2):
                h = 2 * stage + i
                att = within[rows, head(h)] + contract(aq[rows, head(h)], state[h], 1, 0)
                total = total + att * att
                gathered[0, stage, rows, head(i)] = (att * gate[rows, head(h)]).astype(BF16)
            squares[rows, :] = total
            chunk = 2 * stage + part
            slot_send(chunk, 1, chunk, True).start()
            slot_send(chunk, 1, chunk, False).start()

    finish_state(0)
    finish_attended(0)
    finish_state(1)
    finish_attended(1)
    ss_own[...] = jnp.zeros_like(ss_own)
    for group in range(ROWS // 128):
        tile = squares[group * 128 : (group + 1) * 128, :]
        ss_own[group : group + 1, :] = jnp.sum(tile.T, axis=0, keepdims=True)

    square_sends = []
    for step in range(1, NZ):
        copy = remote(
            ss_own, ss_all.at[step - 1], ss_send.at[step - 1], ss_recv.at[step - 1], z_peer(step)
        )
        copy.start()
        square_sends.append(copy)

    others = pl.ds(1, NZ - 1)
    for copy in weight_z:
        copy.wait_recv()

    def share_rows(step):
        return pl.ds(pl.multiple_of(c * 256 + b * 64 + lax.rem(a + step, NX) * 16, 16), 16)

    def group_rows(step):
        return pl.ds(pl.multiple_of(c * 256 + lax.rem(b + step, NX) * 64, 64), 64)

    def ring_starts(rows, peer, send_sem, recv_sem):
        piece = weight.at[others, rows(0)]
        up = remote(piece, piece, send_sem.at[0], recv_sem.at[0], peer(1))
        down = remote(piece, piece, send_sem.at[1], recv_sem.at[1], peer(NX - 1))
        up.start()
        down.start()
        return [up, down]

    def ring_forwards(rows, peer, send_sem, recv_sem, copies):
        copies[0].wait_recv()
        from_below = weight.at[others, rows(NX - 1), pl.ds(0, HALF)]
        up = remote(from_below, from_below, send_sem.at[2], recv_sem.at[2], peer(1))
        up.start()
        copies[1].wait_recv()
        from_above = weight.at[others, rows(1), pl.ds(HALF, HALF)]
        down = remote(from_above, from_above, send_sem.at[3], recv_sem.at[3], peer(NX - 1))
        down.start()
        return [up, down]

    ring_a = ring_starts(share_rows, a_peer, wa_send, wa_recv)

    def project(slot, row, count, fresh=False):
        rows = pl.ds(pl.multiple_of(row, 128), count)
        for n in range(OUT // 256):
            cols = slice(n * 256, (n + 1) * 256)
            term = contract(gathered[slot, 0, rows, :], weight[slot, 0:PAIR, cols], 1, 0)
            term = term + contract(gathered[slot, 1, rows, :], weight[slot, PAIR:FEAT, cols], 1, 0)
            if fresh:
                acc[rows, cols] = term
            else:
                acc[rows, cols] += term

    load_w.wait()
    for part in range(2):
        project(0, part * 256, 256, fresh=True)

    def pass_on(index, _):
        hop = lax.div(index, NCHUNK) + 1
        chunk = lax.rem(index, NCHUNK)
        slot_send(index, hop, chunk, True).wait_recv()
        slot_send(index + NCHUNK, hop + 1, chunk, True).start()
        slot_send(index, hop, chunk, False).wait_recv()
        slot_send(index + NCHUNK, hop + 1, chunk, False).start()
        return 0

    def pass_range(start, stop):
        lax.fori_loop(start, stop, pass_on, 0)

    pass_range(0, 1)
    ring_a2 = ring_forwards(share_rows, a_peer, wa_send, wa_recv, ring_a)
    pass_range(1, 2)
    for copy in ring_a2:
        copy.wait_recv()
    ring_b = ring_starts(group_rows, b_peer, wb_send, wb_recv)

    def to_sibling(step):
        piece = weight.at[others, group_rows(step)]
        copy = remote(piece, piece, ws_send.at[step], ws_recv.at[step], sibling)
        copy.start()
        return copy

    sibling_sends = [to_sibling(0)]
    pass_range(2, 5)
    ring_b2 = ring_forwards(group_rows, b_peer, wb_send, wb_recv, ring_b)
    sibling_sends.append(to_sibling(1))
    sibling_sends.append(to_sibling(3))
    pass_range(5, 7)
    for copy in ring_b2:
        copy.wait_recv()
    sibling_sends.append(to_sibling(2))
    pass_range(7, 8)
    for copy in sibling_sends:
        copy.wait_recv()

    def hop_three(chunk):
        index = 2 * NCHUNK + chunk
        slot_send(index, 3, chunk, True).wait_recv()
        if chunk < NCHUNK // 2:
            slot_send(index + NCHUNK, 4, chunk, True).start()
        slot_send(index, 3, chunk, False).wait_recv()
        if chunk >= NCHUNK // 2:
            slot_send(index + NCHUNK, 4, chunk, False).start()

    def project_whole(slot):
        def body(part, _):
            project(slot, part * 256, 256)
            return 0
        lax.fori_loop(0, 2, body, 0)

    hop_three(0)
    project_whole(7)
    hop_three(1)
    project_whole(1)
    hop_three(2)
    project_whole(6)
    hop_three(3)
    project_whole(2)
    project_whole(5)
    project_whole(3)

    for step in range(NZ - 1):
        square_sends[step].wait_recv()
    sums = ss_own[...]
    for step in range(NZ - 1):
        sums = sums + ss_all[step]
    factor = lax.rsqrt(sums / (HEADS * HEAD_DIM) + 1e-06)

    for part in range(2):
        slot_send(3 * NCHUNK + part, 4, part, True).wait_recv()
        slot_send(3 * NCHUNK + part + 2, 4, part + 2, False).wait_recv()
        project(4, part * half, half)
        for group in (2 * part, 2 * part + 1):
            rows = slice(group * 128, (group + 1) * 128)
            column = jnp.broadcast_to(factor[group : group + 1, :], (128, 128)).T
            for n in range(OUT // 128):
                cols = slice(n * 128, (n + 1) * 128)
                out_ref[rows, cols] = (acc[rows, cols] * column).astype(BF16)

    @pl.when(c == 0)
    def _():
        for stage in range(2):
            to_core1(stage).wait_send()

    @pl.when(c == 1)
    def _():
        for stage in range(2):
            to_core0(stage).wait_send()
        for h in range(4):
            for step in range(1, NX):
                first_phase(h, step).wait_send()
                second_phase(h, step).wait_send()

    for copy in (
        weight_z + square_sends + ring_a + ring_a2 + ring_b + ring_b2 + sibling_sends
    ):
        copy.wait_send()

    def drain(index, _):
        hop = lax.div(index, NCHUNK) + 1
        chunk = lax.rem(index, NCHUNK)
        slot_send(index, hop, chunk, True).wait_send()
        slot_send(index, hop, chunk, False).wait_send()
        return 0

    lax.fori_loop(0, 3 * NCHUNK, drain, 0)
    for chunk in range(NCHUNK):
        slot_send(3 * NCHUNK + chunk, 4, chunk, chunk < NCHUNK // 2).wait_send()


def body(*arrays):
    dma = pltpu.SemaphoreType.DMA
    full = (4, HEAD_DIM, HEAD_DIM)
    vmem = pltpu.VMEM
    return pl.pallas_call(
        kernel,
        out_shape=jax.ShapeDtypeStruct((ROWS, OUT), BF16),
        in_specs=[pl.BlockSpec(memory_space=pl.ANY)] * 5,
        out_specs=pl.BlockSpec(memory_space=pltpu.VMEM),
        scratch_shapes=[
            vmem((ROWS, FEAT), BF16), vmem((ROWS, FEAT), BF16),
            vmem((ROWS, FEAT), BF16), vmem((ROWS, FEAT), BF16),
            vmem((ROWS, FEAT), BF16), vmem((ROWS, FEAT), BF16), vmem((ROWS, FEAT), BF16),
            vmem((ROWS, FEAT), F32), vmem((ROWS, FEAT), F32), vmem((ROWS, HEAD_DIM), F32),
            vmem(full, F32), vmem(full, BF16), vmem(full, BF16), vmem(full, BF16), vmem(full, F32),
            vmem((4, NX - 1, HEAD_DIM, HEAD_DIM), BF16), vmem((4, 2, HEAD_DIM, HEAD_DIM), BF16),
            vmem((4, NX - 1, HEAD_DIM, HEAD_DIM), BF16), vmem(full, BF16), vmem(full, BF16),
            vmem((NZ, 2, ROWS, PAIR), BF16), vmem((NZ, ROWS, OUT), BF16),
            vmem((ROWS, OUT), F32), vmem((8, 128), F32), vmem((NZ - 1, 8, 128), F32),
            dma((7,)), dma((NZ - 1,)), dma((NZ - 1,)), dma((4,)), dma((4,)),
            dma((12,)), dma((12,)), dma((12,)), dma((12,)),
            dma((NZ - 1,)), dma((NZ - 1,)),
            dma((4 * NCHUNK,)), dma((4 * NCHUNK,)), dma((4 * NCHUNK,)), dma((4 * NCHUNK,)),
            dma((4,)), dma((4,)), dma((4,)), dma((4,)), dma((4,)), dma((4,)),
        ],
        compiler_params=pltpu.CompilerParams(
            collective_id=0, has_side_effects=True, vmem_limit_bytes=48 * 1024 * 1024
        ),
        cost_estimate=pl.CostEstimate(
            flops=3_900_000_000, bytes_accessed=9_000_000, transcendentals=1_000_000
        ),
    )(*(pltpu.with_memory_space_constraint(arg, pltpu.HBM) for arg in arrays))


def solution(mesh):
    return jax.shard_map(
        body,
        mesh=mesh,
        in_specs=(
            P("seq", "head"),
            P("seq", "head"),
            P("seq", "head"),
            P("seq", "head"),
            P("head", None),
        ),
        out_specs=P("seq", "head"),
        check_vma=False,
    )
```

time: 71.2 us -> 62.7 us (0.88)
  local copies, waits for them, and re-layouts: 5.05 us -> 0.88 us
  Pallas kernels: 65.8 us -> 61.7 us
    unnamed x9 -> x1, local copies, waits for them, and re-layouts: 5.05 us -> 0.88 us
    pallas_call x1, Pallas kernels: 65.8 us -> 61.7 us  [body(): pl.pallas_call(kernel, out_shape=jax.ShapeDtypeStruct((ROWS, OUT), BF16),...]
where the time goes in v2:
time: 62.7 us; the launch traced here: 62.6 us
  Pallas kernels  61.7 us (98%)
  local copies, waits for them, and re-layouts  0.88 us (1%)
    pallas_call x1, Pallas kernels, body(): pl.pallas_call(kernel, out_shape=jax.ShapeDtypeStruct((ROWS, OUT), BF16),...  61.7 us

profile of v2, /device:TPU:1, one launch (start us, length us, event | category | flops | bytes accessed | tf_op | source)
XLA Modules:
  0.0 62.6 jit_solution(13997576707498864588)
XLA Ops:
  0.0 61.7 %shard_map.55 = bf16[512,768]{1,0:T(8,128)(2,1)S(1)} custom-call(bf16[512,512]{1,0:T(8,128)(2,1)} %q_hbm.1, bf16[512,512]{1,0:T(8,128)(2,1)} %k_hbm.1, bf16[512,512]{1,0:T(8,128)(2,1)} %v_hbm.1, bf16[512,512]{1,0:T(8,128)(2,1)} %g_hbm.1, bf16[512,6144]{1,0:T(8,128)(2,1)} %w_hbm.1), custom_call_target="tpu_custom_call" | custom-call | flops 3900000000 | bytes 9000000 | tf_op jit(solution)/shard_map/pallas_call | solution.py:454
  61.7 0.9 %copy.7 = bf16[512,768]{1,0:T(8,128)(2,1)} copy(bf16[512,768]{1,0:T(8,128)(2,1)S(1)} %shard_map.55) | data formatting | bytes 1572864

commit v3 on v2

--- a/solution.py
+++ b/solution.py
@@ -15,6 +15,7 @@
 
 NX = 4
 NZ = 8
+STEPS = (2, 1, 3)
 ROWS = 512
 FEAT = 512
 OUT = 768
@@ -43,7 +44,7 @@
     q_in, k_in, v_in, g_in, aq, ak, av, within, gate, squares,
     s_full, s_bf, sib, tot_bf, low_sum, arr_a, pay, arr_b, back, state,
     gathered, weight, acc, ss_own, ss_all,
-    load_sem, z_send, z_recv, p_send, p_recv, a_send, a_recv, b_send, b_recv,
+    near, load_sem, z_send, z_recv, p_send, p_recv, a_send, a_recv, b_send, b_recv,
     ss_send, ss_recv, r_send, r_recv, l_send, l_recv,
     wa_send, wa_recv, wb_send, wb_recv, ws_send, ws_recv,
 ):
@@ -82,7 +83,7 @@
         [sibling]
         + [chip(step, 0) for step in range(1, NX)]
         + [chip(0, step) for step in range(1, NX)]
-        + [z_peer(step) for step in range(1, NZ)]
+        + [z_peer(1), z_peer(NZ - 1)]
     )
     for partner in partners:
         pl.semaphore_signal(barrier, inc=1, device_id=partner, device_id_type=MESH)
@@ -138,32 +139,45 @@
             b_send.at[index], b_recv.at[index], device,
         )
 
-    def local_states(stage):
-        for copy in loads_kv[stage]:
-            copy.wait()
+    def local_state(h):
+        ak[:, head(h)] = silu(k_in[:, head(h)])
+        av[:, head(h)] = silu(v_in[:, head(h)])
+        outer = contract(ak[:, head(h)], av[:, head(h)], 0, 0)
+        s_full[h] = outer
+        s_bf[h] = outer.astype(BF16)
+
+    def depart(stage):
+        to_core1(stage).wait_recv()
         for h in (2 * stage, 2 * stage + 1):
-            ak[:, head(h)] = silu(k_in[:, head(h)])
-            av[:, head(h)] = silu(v_in[:, head(h)])
-            outer = contract(ak[:, head(h)], av[:, head(h)], 0, 0)
-            s_full[h] = outer
-            s_bf[h] = outer.astype(BF16)
-
-    local_states(0)
+            tot_bf[h] = (s_full[h] + sib[h].astype(F32)).astype(BF16)
+            for step in STEPS:
+                first_phase(h, step).start()
+
+    def greet(index, distance):
+        for step in (distance, NZ - distance):
+            pl.semaphore_signal(
+                near.at[index], inc=1, device_id=z_peer(step), device_id_type=MESH
+            )
+
+    for copy in loads_kv[0]:
+        copy.wait()
+    local_state(0)
+    local_state(1)
     pl.semaphore_wait(barrier, len(partners))
     pl.when(c == 0)(lambda: to_core1(0).start())
-    local_states(1)
+    greet(0, 1)
+    for copy in loads_kv[1]:
+        copy.wait()
+    local_state(2)
+    pl.when(c == 1)(lambda: depart(0))
+    pl.semaphore_wait(near.at[0], 2)
+    greet(1, 2)
+    local_state(3)
     pl.when(c == 0)(lambda: to_core1(1).start())
-
-    @pl.when(c == 1)
-    def _():
-        for stage in range(2):
-            to_core1(stage).wait_recv()
-            for h in (2 * stage, 2 * stage + 1):
-                tot_bf[h] = (s_full[h] + sib[h].astype(F32)).astype(BF16)
-                for step in range(1, NX):
-                    first_phase(h, step).start()
+    pl.when(c == 1)(lambda: depart(1))
 
     share = pl.multiple_of(c * 256 + b * 64 + a * 16, 16)
+    pl.semaphore_wait(near.at[1], 2)
     weight_z = []
     for step in range(1, NZ):
         columns = pl.ds(pl.multiple_of(lax.rem(z + step, NZ) * OUT, 128), OUT)
@@ -216,7 +230,7 @@
             else:
                 pay[h, 0] = (lower + total).astype(BF16)
                 pay[h, 1] = lower.astype(BF16)
-            for step in range(1, NX):
+            for step in STEPS:
                 second_phase(h, step).start()
 
     pl.when(c == 1)(lambda: turn(0))
@@ -289,8 +303,6 @@
         square_sends.append(copy)
 
     others = pl.ds(1, NZ - 1)
-    for copy in weight_z:
-        copy.wait_recv()
 
     def share_rows(step):
         return pl.ds(pl.multiple_of(c * 256 + b * 64 + lax.rem(a + step, NX) * 16, 16), 16)
@@ -317,7 +329,6 @@
         down.start()
         return [up, down]
 
-    ring_a = ring_starts(share_rows, a_peer, wa_send, wa_recv)
 
     def project(slot, row, count, fresh=False):
         rows = pl.ds(pl.multiple_of(row, 128), count)
@@ -346,6 +357,9 @@
     def pass_range(start, stop):
         lax.fori_loop(start, stop, pass_on, 0)
 
+    for copy in weight_z:
+        copy.wait_recv()
+    ring_a = ring_starts(share_rows, a_peer, wa_send, wa_recv)
     pass_range(0, 1)
     ring_a2 = ring_forwards(share_rows, a_peer, wa_send, wa_recv, ring_a)
     pass_range(1, 2)
@@ -364,11 +378,10 @@
     ring_b2 = ring_forwards(group_rows, b_peer, wb_send, wb_recv, ring_b)
     sibling_sends.append(to_sibling(1))
     sibling_sends.append(to_sibling(3))
-    pass_range(5, 7)
+    pass_range(5, 8)
     for copy in ring_b2:
         copy.wait_recv()
     sibling_sends.append(to_sibling(2))
-    pass_range(7, 8)
     for copy in sibling_sends:
         copy.wait_recv()
 
@@ -466,7 +479,7 @@
             vmem((4, NX - 1, HEAD_DIM, HEAD_DIM), BF16), vmem(full, BF16), vmem(full, BF16),
             vmem((NZ, 2, ROWS, PAIR), BF16), vmem((NZ, ROWS, OUT), BF16),
             vmem((ROWS, OUT), F32), vmem((8, 128), F32), vmem((NZ - 1, 8, 128), F32),
-            dma((7,)), dma((NZ - 1,)), dma((NZ - 1,)), dma((4,)), dma((4,)),
+            pltpu.SemaphoreType.REGULAR((2,)), dma((7,)), dma((NZ - 1,)), dma((NZ - 1,)), dma((4,)), dma((4,)),
             dma((12,)), dma((12,)), dma((12,)), dma((12,)),
             dma((NZ - 1,)), dma((NZ - 1,)),
             dma((4 * NCHUNK,)), dma((4 * NCHUNK,)), dma((4 * NCHUNK,)), dma((4 * NCHUNK,)),

time: 62.7 us -> 61.4 us (0.979)
  Pallas kernels: 61.7 us -> 60.5 us
    pallas_call x1, Pallas kernels: 61.7 us -> 60.5 us  [body(): pl.pallas_call(kernel, out_shape=jax.ShapeDtypeStruct((ROWS, OUT), BF16),...]
where the time goes in v3:
time: 61.4 us; the launch traced here: 61.3 us
  Pallas kernels  60.5 us (99%)
  local copies, waits for them, and re-layouts  0.88 us (1%)
    pallas_call x1, Pallas kernels, body(): pl.pallas_call(kernel, out_shape=jax.ShapeDtypeStruct((ROWS, OUT), BF16),...  60.5 us

profile of v3, /device:TPU:1, one launch (start us, length us, event | category | flops | bytes accessed | tf_op | source)
XLA Modules:
  0.0 61.3 jit_solution(13755542534702757625)
XLA Ops:
  0.0 60.5 %shard_map.55 = bf16[512,768]{1,0:T(8,128)(2,1)S(1)} custom-call(bf16[512,512]{1,0:T(8,128)(2,1)} %q_hbm.1, bf16[512,512]{1,0:T(8,128)(2,1)} %k_hbm.1, bf16[512,512]{1,0:T(8,128)(2,1)} %v_hbm.1, bf16[512,512]{1,0:T(8,128)(2,1)} %g_hbm.1, bf16[512,6144]{1,0:T(8,128)(2,1)} %w_hbm.1), custom_call_target="tpu_custom_call" | custom-call | flops 3900000000 | bytes 9000000 | tf_op jit(solution)/shard_map/pallas_call | solution.py:467
  60.5 0.9 %copy.7 = bf16[512,768]{1,0:T(8,128)(2,1)} copy(bf16[512,768]{1,0:T(8,128)(2,1)S(1)} %shard_map.55) | data formatting | bytes 1572864

commit v4 on v3

--- a/solution.py
+++ b/solution.py
@@ -103,10 +103,6 @@
             load(k_hbm.at[:, part], k_in.at[:, part], 2 * stage),
             load(v_hbm.at[:, part], v_in.at[:, part], 2 * stage + 1),
         ))
-    load_q = load(q_hbm, q_in, 4)
-    load_g = load(g_hbm, g_in, 5)
-    own_columns = pl.ds(pl.multiple_of(z * OUT, 128), OUT)
-    load_w = load(w_hbm.at[:, own_columns], weight.at[0], 6)
 
     def stage_heads(stage):
         return pl.ds(2 * stage, 2)
@@ -133,11 +129,31 @@
     def second_phase(h, step):
         index = h * (NX - 1) + step - 1
         device = chip(0, step) if h % 2 == 0 else chip(step, 0)
-        place = y if h % 2 == 0 else x
+        piece = 0 if h % 2 == 0 else lax.div(x + step, NX)
         return remote(
-            pay.at[h, lax.div(place + step, NX)], arr_b.at[h, step - 1],
+            pay.at[h, piece], arr_b.at[h, step - 1],
             b_send.at[index], b_recv.at[index], device,
         )
+
+    def first_sends(h, step):
+        if h % 2 == 0:
+            return jnp.logical_or(x + step < NX, y < NX - 1)
+        return y + step < NX
+
+    def first_hears(h, step):
+        if h % 2 == 0:
+            return jnp.logical_or(x >= step, y < NX - 1)
+        return y >= step
+
+    def second_sends(h, step):
+        if h % 2 == 0:
+            return y + step < NX
+        return jnp.logical_or(x + step < NX, y > 0)
+
+    def second_hears(h, step):
+        if h % 2 == 0:
+            return y >= step
+        return jnp.logical_or(x >= step, y > 0)
 
     def local_state(h):
         ak[:, head(h)] = silu(k_in[:, head(h)])
@@ -151,7 +167,7 @@
         for h in (2 * stage, 2 * stage + 1):
             tot_bf[h] = (s_full[h] + sib[h].astype(F32)).astype(BF16)
             for step in STEPS:
-                first_phase(h, step).start()
+                pl.when(first_sends(h, step))(first_phase(h, step).start)
 
     def greet(index, distance):
         for step in (distance, NZ - distance):
@@ -161,6 +177,7 @@
 
     for copy in loads_kv[0]:
         copy.wait()
+    load_q = load(q_hbm, q_in, 4)
     local_state(0)
     local_state(1)
     pl.semaphore_wait(barrier, len(partners))
@@ -168,6 +185,7 @@
     greet(0, 1)
     for copy in loads_kv[1]:
         copy.wait()
+    load_g = load(g_hbm, g_in, 5)
     local_state(2)
     pl.when(c == 1)(lambda: depart(0))
     pl.semaphore_wait(near.at[0], 2)
@@ -209,29 +227,49 @@
     load_q.wait()
     for h in range(4):
         aq[:, head(h)] = silu(q_in[:, head(h)])
+    own_columns = pl.ds(pl.multiple_of(z * OUT, 128), OUT)
+    load_w = load(w_hbm.at[:, own_columns], weight.at[0], 6)
     attend_block(0)
     attend_block(1)
 
+    def add_term(copy, term, h):
+        copy.wait_recv()
+        low_sum[h] += term[...].astype(F32)
+
     def turn(stage):
         for h in (2 * stage, 2 * stage + 1):
-            place = x if h % 2 == 0 else y
             total = s_full[h] + sib[h].astype(F32)
-            lower = jnp.zeros((HEAD_DIM, HEAD_DIM), F32)
-            whole = total
-            for step in range(1, NX):
-                first_phase(h, step).wait_recv()
-                term = arr_a[h, step - 1].astype(F32)
-                lower = lower + term * jnp.where(place >= step, 1.0, 0.0).astype(F32)
-                whole = whole + term
-            low_sum[h] = lower
+            low_sum[h] = jnp.zeros((HEAD_DIM, HEAD_DIM), F32)
             if h % 2 == 0:
-                pay[h, 0] = whole.astype(BF16)
-                pay[h, 1] = jnp.zeros((HEAD_DIM, HEAD_DIM), BF16)
+                pay[h, 0] = total.astype(BF16)
+
+                @pl.when(y < NX - 1)
+                def _(h=h, total=total):
+                    lower = jnp.zeros((HEAD_DIM, HEAD_DIM), F32)
+                    whole = total
+                    for step in range(1, NX):
+                        first_phase(h, step).wait_recv()
+                        term = arr_a[h, step - 1].astype(F32)
+                        lower = lower + term * jnp.where(x >= step, 1.0, 0.0).astype(F32)
+                        whole = whole + term
+                    low_sum[h] = lower
+                    pay[h, 0] = whole.astype(BF16)
+
+                @pl.when(y == NX - 1)
+                def _(h=h):
+                    for step in range(1, NX):
+                        pl.when(x >= step)(functools.partial(
+                            add_term, first_phase(h, step), arr_a.at[h, step - 1], h
+                        ))
             else:
-                pay[h, 0] = (lower + total).astype(BF16)
-                pay[h, 1] = lower.astype(BF16)
+                for step in range(1, NX):
+                    pl.when(first_hears(h, step))(functools.partial(
+                        add_term, first_phase(h, step), arr_a.at[h, step - 1], h
+                    ))
+                pay[h, 0] = (low_sum[h] + total).astype(BF16)
+                pay[h, 1] = low_sum[h].astype(BF16)
             for step in STEPS:
-                second_phase(h, step).start()
+                pl.when(second_sends(h, step))(second_phase(h, step).start)
 
     pl.when(c == 1)(lambda: turn(0))
     attend_block(2)
@@ -245,10 +283,11 @@
         @pl.when(c == 1)
         def _():
             for h in (2 * stage, 2 * stage + 1):
+                for step in range(1, NX):
+                    pl.when(second_hears(h, step))(functools.partial(
+                        add_term, second_phase(h, step), arr_b.at[h, step - 1], h
+                    ))
                 before = low_sum[h]
-                for step in range(1, NX):
-                    second_phase(h, step).wait_recv()
-                    before = before + arr_b[h, step - 1].astype(F32)
                 back[h] = before.astype(BF16)
                 state[h] = (before + sib[h].astype(F32)).astype(BF16)
             to_core0(stage).start()
@@ -289,7 +328,6 @@
     finish_attended(0)
     finish_state(1)
     finish_attended(1)
-    ss_own[...] = jnp.zeros_like(ss_own)
     for group in range(ROWS // 128):
         tile = squares[group * 128 : (group + 1) * 128, :]
         ss_own[group : group + 1, :] = jnp.sum(tile.T, axis=0, keepdims=True)
@@ -440,8 +478,8 @@
             to_core0(stage).wait_send()
         for h in range(4):
             for step in range(1, NX):
-                first_phase(h, step).wait_send()
-                second_phase(h, step).wait_send()
+                pl.when(first_sends(h, step))(first_phase(h, step).wait_send)
+                pl.when(second_sends(h, step))(second_phase(h, step).wait_send)
 
     for copy in (
         weight_z + square_sends + ring_a + ring_a2 + ring_b + ring_b2 + sibling_sends
@@ -478,7 +516,7 @@
             vmem((4, NX - 1, HEAD_DIM, HEAD_DIM), BF16), vmem((4, 2, HEAD_DIM, HEAD_DIM), BF16),
             vmem((4, NX - 1, HEAD_DIM, HEAD_DIM), BF16), vmem(full, BF16), vmem(full, BF16),
             vmem((NZ, 2, ROWS, PAIR), BF16), vmem((NZ, ROWS, OUT), BF16),
-            vmem((ROWS, OUT), F32), vmem((8, 128), F32), vmem((NZ - 1, 8, 128), F32),
+            vmem((ROWS, OUT), F32), vmem((4, 128), F32), vmem((NZ - 1, 4, 128), F32),
             pltpu.SemaphoreType.REGULAR((2,)), dma((7,)), dma((NZ - 1,)), dma((NZ - 1,)), dma((4,)), dma((4,)),
             dma((12,)), dma((12,)), dma((12,)), dma((12,)),
             dma((NZ - 1,)), dma((NZ - 1,)),

time: 61.4 us -> 60.7 us (0.989)
  Pallas kernels: 60.5 us -> 59.2 us
    pallas_call x1, Pallas kernels: 60.5 us -> 59.2 us  [body(): pl.pallas_call(kernel, out_shape=jax.ShapeDtypeStruct((ROWS, OUT), BF16),...]
where the time goes in v4:
time: 60.7 us; the launch traced here: 60.1 us
  Pallas kernels  59.2 us (98%)
  local copies, waits for them, and re-layouts  0.88 us (1%)
    pallas_call x1, Pallas kernels, body(): pl.pallas_call(kernel, out_shape=jax.ShapeDtypeStruct((ROWS, OUT), BF16),...  59.2 us

profile of v4, /device:TPU:1, one launch (start us, length us, event | category | flops | bytes accessed | tf_op | source)
XLA Modules:
  0.0 60.1 jit_solution(552008849865212482)
XLA Ops:
  0.0 59.2 %shard_map.55 = bf16[512,768]{1,0:T(8,128)(2,1)S(1)} custom-call(bf16[512,512]{1,0:T(8,128)(2,1)} %q_hbm.1, bf16[512,512]{1,0:T(8,128)(2,1)} %k_hbm.1, bf16[512,512]{1,0:T(8,128)(2,1)} %v_hbm.1, bf16[512,512]{1,0:T(8,128)(2,1)} %g_hbm.1, bf16[512,6144]{1,0:T(8,128)(2,1)} %w_hbm.1), custom_call_target="tpu_custom_call" | custom-call | flops 3900000000 | bytes 9000000 | tf_op jit(solution)/shard_map/pallas_call | solution.py:505
  59.3 0.9 %copy.7 = bf16[512,768]{1,0:T(8,128)(2,1)} copy(bf16[512,768]{1,0:T(8,128)(2,1)S(1)} %shard_map.55) | data formatting | bytes 1572864

commit v5 on v4

--- a/solution.py
+++ b/solution.py
@@ -230,7 +230,6 @@
     own_columns = pl.ds(pl.multiple_of(z * OUT, 128), OUT)
     load_w = load(w_hbm.at[:, own_columns], weight.at[0], 6)
     attend_block(0)
-    attend_block(1)
 
     def add_term(copy, term, h):
         copy.wait_recv()
@@ -272,6 +271,7 @@
                 pl.when(second_sends(h, step))(second_phase(h, step).start)
 
     pl.when(c == 1)(lambda: turn(0))
+    attend_block(1)
     attend_block(2)
     pl.when(c == 1)(lambda: turn(1))
     attend_block(3)
@@ -423,14 +423,30 @@
     for copy in sibling_sends:
         copy.wait_recv()
 
+    def last_hop(unit, up):
+        chunk = unit // 2
+        rows = pl.ds((chunk % 2) * half + (unit % 2) * 128, 128)
+        src, sends, recvs, device = (
+            (5, r_send, r_recv, z_peer(1)) if up else (3, l_send, l_recv, z_peer(NZ - 1))
+        )
+        index = 3 * NCHUNK + unit
+        return remote(
+            gathered.at[src, chunk // 2, rows], gathered.at[4, chunk // 2, rows],
+            sends.at[index], recvs.at[index], device,
+        )
+
     def hop_three(chunk):
         index = 2 * NCHUNK + chunk
+        units = (2 * chunk, 2 * chunk + 1)
+        up = units[1] < NCHUNK
         slot_send(index, 3, chunk, True).wait_recv()
-        if chunk < NCHUNK // 2:
-            slot_send(index + NCHUNK, 4, chunk, True).start()
+        if up:
+            for unit in units:
+                last_hop(unit, True).start()
         slot_send(index, 3, chunk, False).wait_recv()
-        if chunk >= NCHUNK // 2:
-            slot_send(index + NCHUNK, 4, chunk, False).start()
+        if not up:
+            for unit in units:
+                last_hop(unit, False).start()
 
     def project_whole(slot):
         def body(part, _):
@@ -456,16 +472,15 @@
         sums = sums + ss_all[step]
     factor = lax.rsqrt(sums / (HEADS * HEAD_DIM) + 1e-06)
 
-    for part in range(2):
-        slot_send(3 * NCHUNK + part, 4, part, True).wait_recv()
-        slot_send(3 * NCHUNK + part + 2, 4, part + 2, False).wait_recv()
-        project(4, part * half, half)
-        for group in (2 * part, 2 * part + 1):
-            rows = slice(group * 128, (group + 1) * 128)
-            column = jnp.broadcast_to(factor[group : group + 1, :], (128, 128)).T
-            for n in range(OUT // 128):
-                cols = slice(n * 128, (n + 1) * 128)
-                out_ref[rows, cols] = (acc[rows, cols] * column).astype(BF16)
+    for group in range(ROWS // 128):
+        last_hop(group, True).wait_recv()
+        last_hop(group + NCHUNK, False).wait_recv()
+        project(4, group * 128, 128)
+        rows = slice(group * 128, (group + 1) * 128)
+        column = jnp.broadcast_to(factor[group : group + 1, :], (128, 128)).T
+        for n in range(OUT // 128):
+            cols = slice(n * 128, (n + 1) * 128)
+            out_ref[rows, cols] = (acc[rows, cols] * column).astype(BF16)
 
     @pl.when(c == 0)
     def _():
@@ -494,8 +509,8 @@
         return 0
 
     lax.fori_loop(0, 3 * NCHUNK, drain, 0)
-    for chunk in range(NCHUNK):
-        slot_send(3 * NCHUNK + chunk, 4, chunk, chunk < NCHUNK // 2).wait_send()
+    for unit in range(2 * NCHUNK):
+        last_hop(unit, unit < NCHUNK).wait_send()
 
 
 def body(*arrays):
@@ -520,7 +535,7 @@
             pltpu.SemaphoreType.REGULAR((2,)), dma((7,)), dma((NZ - 1,)), dma((NZ - 1,)), dma((4,)), dma((4,)),
             dma((12,)), dma((12,)), dma((12,)), dma((12,)),
             dma((NZ - 1,)), dma((NZ - 1,)),
-            dma((4 * NCHUNK,)), dma((4 * NCHUNK,)), dma((4 * NCHUNK,)), dma((4 * NCHUNK,)),
+            dma((5 * NCHUNK,)), dma((5 * NCHUNK,)), dma((5 * NCHUNK,)), dma((5 * NCHUNK,)),
             dma((4,)), dma((4,)), dma((4,)), dma((4,)), dma((4,)), dma((4,)),
         ],
         compiler_params=pltpu.CompilerParams(

time: 60.7 us -> 60.7 us (level)
  no operation moved by 1% of the time
where the time goes in v5:
time: 60.7 us; the launch traced here: 60.1 us
  Pallas kernels  59.3 us (98%)
  local copies, waits for them, and re-layouts  0.88 us (1%)
    pallas_call x1, Pallas kernels, body(): pl.pallas_call(kernel, out_shape=jax.ShapeDtypeStruct((ROWS, OUT), BF16),...  59.3 us

profile of v5, /device:TPU:1, one launch (start us, length us, event | category | flops | bytes accessed | tf_op | source)
XLA Modules:
  0.0 60.1 jit_solution(8507867252344928048)
XLA Ops:
  0.0 59.3 %shard_map.55 = bf16[512,768]{1,0:T(8,128)(2,1)S(1)} custom-call(bf16[512,512]{1,0:T(8,128)(2,1)} %q_hbm.1, bf16[512,512]{1,0:T(8,128)(2,1)} %k_hbm.1, bf16[512,512]{1,0:T(8,128)(2,1)} %v_hbm.1, bf16[512,512]{1,0:T(8,128)(2,1)} %g_hbm.1, bf16[512,6144]{1,0:T(8,128)(2,1)} %w_hbm.1), custom_call_target="tpu_custom_call" | custom-call | flops 3900000000 | bytes 9000000 | tf_op jit(solution)/shard_map/pallas_call | solution.py:520
  59.3 0.9 %copy.7 = bf16[512,768]{1,0:T(8,128)(2,1)} copy(bf16[512,768]{1,0:T(8,128)(2,1)S(1)} %shard_map.55) | data formatting | bytes 1572864

commit v6 on v5

--- a/solution.py
+++ b/solution.py
@@ -107,16 +107,13 @@
     def stage_heads(stage):
         return pl.ds(2 * stage, 2)
 
-    def to_core1(stage):
-        return remote(
-            s_bf.at[stage_heads(stage)], sib.at[stage_heads(stage)],
-            p_send.at[stage], p_recv.at[stage], sibling,
-        )
+    def to_core1(h):
+        return remote(s_bf.at[h], sib.at[h], p_send.at[h], p_recv.at[h], sibling)
 
     def to_core0(stage):
         return remote(
             back.at[stage_heads(stage)], state.at[stage_heads(stage)],
-            p_send.at[2 + stage], p_recv.at[2 + stage], sibling,
+            p_send.at[4 + stage], p_recv.at[4 + stage], sibling,
         )
 
     def first_phase(h, step):
@@ -163,8 +160,8 @@
         s_bf[h] = outer.astype(BF16)
 
     def depart(stage):
-        to_core1(stage).wait_recv()
         for h in (2 * stage, 2 * stage + 1):
+            to_core1(h).wait_recv()
             tot_bf[h] = (s_full[h] + sib[h].astype(F32)).astype(BF16)
             for step in STEPS:
                 pl.when(first_sends(h, step))(first_phase(h, step).start)
@@ -179,19 +176,21 @@
         copy.wait()
     load_q = load(q_hbm, q_in, 4)
     local_state(0)
-    local_state(1)
     pl.semaphore_wait(barrier, len(partners))
     pl.when(c == 0)(lambda: to_core1(0).start())
     greet(0, 1)
+    local_state(1)
+    pl.when(c == 0)(lambda: to_core1(1).start())
     for copy in loads_kv[1]:
         copy.wait()
     load_g = load(g_hbm, g_in, 5)
     local_state(2)
+    pl.when(c == 0)(lambda: to_core1(2).start())
     pl.when(c == 1)(lambda: depart(0))
     pl.semaphore_wait(near.at[0], 2)
     greet(1, 2)
     local_state(3)
-    pl.when(c == 0)(lambda: to_core1(1).start())
+    pl.when(c == 0)(lambda: to_core1(3).start())
     pl.when(c == 1)(lambda: depart(1))
 
     share = pl.multiple_of(c * 256 + b * 64 + a * 16, 16)
@@ -484,8 +483,8 @@
 
     @pl.when(c == 0)
     def _():
-        for stage in range(2):
-            to_core1(stage).wait_send()
+        for h in range(4):
+            to_core1(h).wait_send()
 
     @pl.when(c == 1)
     def _():
@@ -532,7 +531,7 @@
             vmem((4, NX - 1, HEAD_DIM, HEAD_DIM), BF16), vmem(full, BF16), vmem(full, BF16),
             vmem((NZ, 2, ROWS, PAIR), BF16), vmem((NZ, ROWS, OUT), BF16),
             vmem((ROWS, OUT), F32), vmem((4, 128), F32), vmem((NZ - 1, 4, 128), F32),
-            pltpu.SemaphoreType.REGULAR((2,)), dma((7,)), dma((NZ - 1,)), dma((NZ - 1,)), dma((4,)), dma((4,)),
+            pltpu.SemaphoreType.REGULAR((2,)), dma((7,)), dma((NZ - 1,)), dma((NZ - 1,)), dma((6,)), dma((6,)),
             dma((12,)), dma((12,)), dma((12,)), dma((12,)),
             dma((NZ - 1,)), dma((NZ - 1,)),
             dma((5 * NCHUNK,)), dma((5 * NCHUNK,)), dma((5 * NCHUNK,)), dma((5 * NCHUNK,)),

time: 60.7 us -> 60.8 us (level)
  no operation moved by 1% of the time
where the time goes in v6:
time: 60.8 us; the launch traced here: 60.7 us
  Pallas kernels  59.9 us (99%)
  local copies, waits for them, and re-layouts  0.88 us (1%)
    pallas_call x1, Pallas kernels, body(): pl.pallas_call(kernel, out_shape=jax.ShapeDtypeStruct((ROWS, OUT), BF16),...  59.9 us

profile of v6, /device:TPU:1, one launch (start us, length us, event | category | flops | bytes accessed | tf_op | source)
XLA Modules:
  0.0 60.7 jit_solution(17940464893789048888)
XLA Ops:
  0.0 59.9 %shard_map.55 = bf16[512,768]{1,0:T(8,128)(2,1)S(1)} custom-call(bf16[512,512]{1,0:T(8,128)(2,1)} %q_hbm.1, bf16[512,512]{1,0:T(8,128)(2,1)} %k_hbm.1, bf16[512,512]{1,0:T(8,128)(2,1)} %v_hbm.1, bf16[512,512]{1,0:T(8,128)(2,1)} %g_hbm.1, bf16[512,6144]{1,0:T(8,128)(2,1)} %w_hbm.1), custom_call_target="tpu_custom_call" | custom-call | flops 3900000000 | bytes 9000000 | tf_op jit(solution)/shard_map/pallas_call | solution.py:519
  59.9 0.9 %copy.7 = bf16[512,768]{1,0:T(8,128)(2,1)} copy(bf16[512,768]{1,0:T(8,128)(2,1)S(1)} %shard_map.55) | data formatting | bytes 1572864
